TPU v7x, 256 devices: a whole 4x4x8 slice. The times are simulated.
256 devices in a mesh: ctx: 32 (over z, x), head: 8 (over y, core).
Axes of the slice: x: 4, y: 4, z: 8, core: 2. Of those that a mesh axis runs over, the one named last changes fastest.
Arguments:
- queries: bfloat16 [16384, 8192], P(('ctx', 'head')), may hold values from -14 to 14
- key_vectors: bfloat16 [16384, 8192], P(('ctx', 'head')), may hold values from -14 to 14
- value_vectors: bfloat16 [16384, 8192], P(('ctx', 'head')), may hold values from -6 to 6
- out_grad: bfloat16 [16384, 8192], P(('ctx', 'head')), may hold values from -6 to 6
- chosen: int32 [32, 3], P('ctx'), may hold values from 0 to 30, as said below
Outputs:
- query_grad: bfloat16 [16384, 8192], P(('ctx', 'head'))
- key_grad: bfloat16 [16384, 8192], P(('ctx', 'head'))
- value_grad: bfloat16 [16384, 8192], P(('ctx', 'head'))
Inputs may be any that keep to these rules, and one draw needn't show every extreme that they name: `chosen`: row b lists min(b, 3) different blocks below b; its first entry is block b - 1 when b >= 1; its other entries equal b and mark unused slots.
All inputs are finite; a program needn't handle non-finite values.
Results may differ from a plain program's by a relative error of at most 0.0099.
Values may be sent and summed in bfloat16 or wider, within the bound.
A program may use at most 128 MiB of HBM per device.

v0:
```python
import jax
import jax.numpy as jnp
from jax import lax
from jax.sharding import PartitionSpec as P

H = 64
HD = 128
BLOCK = 512
TOPK = 3


masked_score = -1e30


def to_pieces(blocks, row_groups, head_groups):
    count, row_total, head_total, width = blocks.shape
    split = blocks.reshape(
        count, row_groups, row_total // row_groups, head_groups, head_total // head_groups, width
    )
    moved = jnp.transpose(split, (3, 1, 0, 2, 4, 5))
    return moved.reshape(
        head_groups * row_groups, count, row_total // row_groups, head_total // head_groups, width
    )


def from_pieces(pieces, row_groups, head_groups):
    piece_total, count, piece_rows, piece_heads, width = pieces.shape
    split = pieces.reshape(head_groups, row_groups, count, piece_rows, piece_heads, width)
    moved = jnp.transpose(split, (2, 1, 3, 0, 4, 5))
    return moved.reshape(count, row_groups * piece_rows, head_groups * piece_heads, width)


def head_terms(
    query_rows, own_keys, own_values, far_keys, far_values, grad_rows, causal, far_visible, scaling
):
    block_size = own_keys.shape[0]
    key_rows = jnp.concatenate([own_keys, far_keys], axis=0)
    value_rows = jnp.concatenate([own_values, far_values], axis=0)
    visible = jnp.concatenate([causal, far_visible], axis=1)
    scores = jnp.dot(query_rows, key_rows.T, preferred_element_type=jnp.float32) * scaling
    scores = jnp.where(visible, scores, masked_score)
    largest = jnp.max(scores, axis=1, keepdims=True)
    totals = jnp.sum(jnp.exp(scores - largest), axis=1, keepdims=True)
    log_total = largest + jnp.log(totals)
    prob_rows = jnp.exp(scores - log_total)
    weights = prob_rows.astype(jnp.bfloat16)
    attended = jnp.dot(weights, value_rows, preferred_element_type=jnp.float32)
    row_delta = jnp.sum(grad_rows.astype(jnp.float32) * attended, axis=1, keepdims=True)
    dprobs = jnp.dot(grad_rows, value_rows.T, preferred_element_type=jnp.float32)
    dscores = (prob_rows * (dprobs - row_delta)).astype(jnp.bfloat16)
    query_part = (jnp.dot(dscores, key_rows, preferred_element_type=jnp.float32) * scaling).astype(
        jnp.bfloat16
    )
    key_part = jnp.dot(dscores.T, query_rows, preferred_element_type=jnp.float32) * scaling
    value_part = jnp.dot(weights.T, grad_rows, preferred_element_type=jnp.float32)
    return (
        query_part,
        key_part[:block_size],
        key_part[block_size:].astype(jnp.bfloat16),
        value_part[:block_size],
        value_part[block_size:].astype(jnp.bfloat16),
    )


def per_device(queries, key_vectors, value_vectors, out_grad, chosen):
    devices = lax.axis_size("ctx")
    position = lax.axis_index("ctx")
    head_count = H // lax.axis_size("head")
    scaling = HD ** (-0.5)
    query_here, key_here, value_here, grad_here = (
        lax.all_to_all(queries, "head", split_axis=1, concat_axis=0, tiled=True),
        lax.all_to_all(key_vectors, "head", split_axis=1, concat_axis=0, tiled=True),
        lax.all_to_all(value_vectors, "head", split_axis=1, concat_axis=0, tiled=True),
        lax.all_to_all(out_grad, "head", split_axis=1, concat_axis=0, tiled=True),
    )
    local_blocks = query_here.shape[0] // BLOCK
    block_shape = (local_blocks, BLOCK, head_count, HD)
    query_blocks = query_here.reshape(block_shape)
    key_blocks = key_here.reshape(block_shape)
    value_blocks = value_here.reshape(block_shape)
    grad_blocks = grad_here.reshape(block_shape)
    head_groups = 1
    key_table, value_table = (
        lax.all_to_all(
            to_pieces(key_blocks, devices, head_groups),
            "ctx",
            split_axis=0,
            concat_axis=0,
            tiled=True,
        ),
        lax.all_to_all(
            to_pieces(value_blocks, devices, head_groups),
            "ctx",
            split_axis=0,
            concat_axis=0,
            tiled=True,
        ),
    )
    piece_shape = key_table.shape[2:]
    key_table = key_table.reshape((devices * local_blocks,) + piece_shape)
    value_table = value_table.reshape((devices * local_blocks,) + piece_shape)
    everyone = lax.all_gather(chosen, "ctx", axis=0, tiled=True)
    block_total = devices * local_blocks
    far_key_pieces, far_value_pieces = (
        lax.all_to_all(
            jnp.take(key_table, everyone, axis=0), "ctx", split_axis=0, concat_axis=0, tiled=True
        ),
        lax.all_to_all(
            jnp.take(value_table, everyone, axis=0), "ctx", split_axis=0, concat_axis=0, tiled=True
        ),
    )
    far_key_blocks = from_pieces(far_key_pieces, devices, head_groups)
    far_value_blocks = from_pieces(far_value_pieces, devices, head_groups)
    positions = jnp.arange(BLOCK, dtype=jnp.int32)
    causal = positions[:, None] >= positions[None, :]
    block_index = position * local_blocks + 0
    far_used = chosen[0] != block_index
    far_visible = jnp.broadcast_to(jnp.repeat(far_used, BLOCK)[None, :], (BLOCK, TOPK * BLOCK))
    far_key_heads = jnp.transpose(far_key_blocks, (2, 0, 1, 3)).reshape(
        head_count, TOPK * BLOCK, HD
    )
    far_value_heads = jnp.transpose(far_value_blocks, (2, 0, 1, 3)).reshape(
        head_count, TOPK * BLOCK, HD
    )

    def per_head(operands):
        return head_terms(
            operands[0],
            operands[1],
            operands[2],
            operands[3],
            operands[4],
            operands[5],
            causal,
            far_visible,
            scaling,
        )

    results = lax.map(
        per_head,
        (
            jnp.swapaxes(query_blocks[0], 0, 1),
            jnp.swapaxes(key_blocks[0], 0, 1),
            jnp.swapaxes(value_blocks[0], 0, 1),
            far_key_heads,
            far_value_heads,
            jnp.swapaxes(grad_blocks[0], 0, 1),
        ),
    )
    query_part, key_mine, key_theirs, value_mine, value_theirs = results
    query_out = [jnp.swapaxes(query_part, 0, 1)]
    key_own = [jnp.swapaxes(key_mine, 0, 1)]
    value_own = [jnp.swapaxes(value_mine, 0, 1)]
    key_far = jnp.transpose(key_theirs.reshape(head_count, TOPK, BLOCK, HD), (1, 2, 0, 3))
    value_far = jnp.transpose(value_theirs.reshape(head_count, TOPK, BLOCK, HD), (1, 2, 0, 3))
    query_grad = jnp.stack(query_out).reshape(local_blocks * BLOCK, head_count * HD)
    key_own_all = jnp.stack(key_own)
    value_own_all = jnp.stack(value_own)
    key_parts, value_parts = (
        lax.all_to_all(
            to_pieces(key_far, devices, head_groups), "ctx", split_axis=0, concat_axis=0, tiled=True
        ),
        lax.all_to_all(
            to_pieces(value_far, devices, head_groups),
            "ctx",
            split_axis=0,
            concat_axis=0,
            tiled=True,
        ),
    )
    item_count = devices * local_blocks * TOPK
    targets = everyone.reshape(item_count)
    owners = jnp.repeat(jnp.arange(block_total, dtype=jnp.int32), TOPK)
    block_ids = jnp.arange(block_total, dtype=jnp.int32)
    selector = ((block_ids[:, None] == targets[None, :]) & (targets != owners)[None, :]).astype(
        jnp.bfloat16
    )
    key_sums = jnp.dot(
        selector, key_parts.reshape(item_count, -1), preferred_element_type=jnp.float32
    )
    value_sums = jnp.dot(
        selector, value_parts.reshape(item_count, -1), preferred_element_type=jnp.float32
    )
    sum_shape = (devices, local_blocks) + piece_shape
    key_back, value_back = (
        lax.all_to_all(key_sums.reshape(sum_shape), "ctx", split_axis=0, concat_axis=0, tiled=True),
        lax.all_to_all(
            value_sums.reshape(sum_shape), "ctx", split_axis=0, concat_axis=0, tiled=True
        ),
    )
    key_total = key_own_all + from_pieces(key_back, devices, head_groups)
    value_total = value_own_all + from_pieces(value_back, devices, head_groups)
    key_grad = key_total.astype(jnp.bfloat16).reshape(local_blocks * BLOCK, head_count * HD)
    value_grad = value_total.astype(jnp.bfloat16).reshape(local_blocks * BLOCK, head_count * HD)
    return (
        lax.all_to_all(query_grad, "head", split_axis=0, concat_axis=1, tiled=True),
        lax.all_to_all(key_grad, "head", split_axis=0, concat_axis=1, tiled=True),
        lax.all_to_all(value_grad, "head", split_axis=0, concat_axis=1, tiled=True),
    )


def solution(mesh):
    placed = (
        P(("ctx", "head"), None),
        P(("ctx", "head"), None),
        P(("ctx", "head"), None),
        P(("ctx", "head"), None),
        P("ctx", None),
    )
    return jax.shard_map(
        per_device,
        mesh=mesh,
        in_specs=placed,
        out_specs=(P(("ctx", "head"), None), P(("ctx", "head"), None), P(("ctx", "head"), None)),
        check_vma=False,
    )
```

profile of v0, /device:TPU:1, one launch (start us, length us, event | category | flops | bytes accessed | tf_op | source)
XLA Modules:
  0.0 944.0 jit_solution(11690668597409902097)
XLA Ops:
  10.8 14.1 %all-to-all-done = bf16[64,8,1024]{2,0,1:T(8,128)(2,1)S(1)} async-done(((bf16[64,8,1024]{2,0,1:T(8,128)(2,1)}), bf16[64,8,1024]{2,0,1:T(8,128)(2,1)S(1)}, u32[]{:S(2)}, u32[]{:S(2)}) %all-to-all-start) | async-done | bytes 1048608 | tf_op jit(solution)/shard_map/all_to_all | solution.py:71
  31.5 12.8 %all-to-all-done.1 = bf16[64,8,1024]{2,0,1:T(8,128)(2,1)S(1)} async-done(((bf16[64,8,1024]{2,0,1:T(8,128)(2,1)}), bf16[64,8,1024]{2,0,1:T(8,128)(2,1)S(1)}, u32[]{:S(2)}, u32[]{:S(2)}) %all-to-all-start.1) | async-done | bytes 1048608 | tf_op jit(solution)/shard_map/all_to_all | solution.py:72
  49.9 13.9 %all-to-all-done.5 = bf16[64,8,1024]{2,0,1:T(8,128)(2,1)S(1)} async-done(((bf16[64,8,1024]{2,0,1:T(8,128)(2,1)}), bf16[64,8,1024]{2,0,1:T(8,128)(2,1)S(1)}, u32[]{:S(2)}, u32[]{:S(2)}) %all-to-all-start.5) | async-done | bytes 1048608 | tf_op jit(solution)/shard_map/all_to_all | solution.py:73
  63.7 10.4 %all-to-all-start.2 = ((bf16[32,1,16,8,128]{4,3,2,1,0:T(8,128)(2,1)}), bf16[32,1,16,8,128]{4,3,2,1,0:T(8,128)(2,1)S(1)}, u32[]{:S(2)}, u32[]{:S(2)}) async-start(bf16[32,1,16,8,128]{4,3,2,1,0:T(8,128)(2,1)} %bitcast.17), calls=%async_computation.2 | async-start | bytes 2097152 | tf_op jit(solution)/shard_map/all_to_all | solution.py:84
  75.4 24.8 %all-to-all-done.2 = bf16[32,1,16,8,128]{4,3,2,1,0:T(8,128)(2,1)S(1)} async-done(((bf16[32,1,16,8,128]{4,3,2,1,0:T(8,128)(2,1)}), bf16[32,1,16,8,128]{4,3,2,1,0:T(8,128)(2,1)S(1)}, u32[]{:S(2)}, u32[]{:S(2)}) %all-to-all-start.2) | async-done | bytes 1048608 | tf_op jit(solution)/shard_map/all_to_all | solution.py:84
  106.5 47.8 %all-gather = s32[32,1,3]{2,1,0:T(1,128)S(1)} all-gather(s32[1,1,3]{2,1,0:T(1,128)S(1)} %bitcast.248), channel_id=1, replica_groups=mesh['ctx'=32,'head'=8] {'ctx'}, dimensions={0}, use_global_device_ids=true | all-gather | bytes 396 | tf_op jit(solution)/shard_map/all_gather | solution.py:102
  155.5 14.2 %all-to-all-start.4 = ((bf16[64,8,1024]{2,0,1:T(8,128)(2,1)}), bf16[64,8,1024]{2,0,1:T(8,128)(2,1)}, u32[]{:S(2)}, u32[]{:S(2)}) async-start(bf16[64,8,1024]{2,0,1:T(8,128)(2,1)} %bitcast.181), calls=%async_computation.4 | async-start | bytes 2097152 | tf_op jit(solution)/shard_map/all_to_all | solution.py:74
  184.9 76.3 %all_to_all.161 = bf16[32,3,16,8,128]{4,3,2,1,0:T(8,128)(2,1)} all-to-all(bf16[32,3,16,8,128]{4,3,2,1,0:T(8,128)(2,1)S(1)} %get-tuple-element.239), channel_id=1, replica_groups=mesh['ctx'=32,'head'=8] {'ctx'}, dimensions={0} | all-to-all | bytes 6291456 | tf_op jit(solution)/shard_map/all_to_all | solution.py:108
  282.1 55.4 %all-to-all-done.3 = bf16[32,3,16,8,128]{4,3,2,1,0:T(8,128)(2,1)} async-done(((bf16[32,3,16,8,128]{4,3,2,1,0:T(8,128)(2,1)}), bf16[32,3,16,8,128]{4,3,2,1,0:T(8,128)(2,1)}, u32[]{:S(2)}, u32[]{:S(2)}) %all-to-all-start.3) | async-done | bytes 3145760 | tf_op jit(solution)/shard_map/all_to_all | solution.py:105
  341.9 268.7 %while.20 = (s32[]{:T(128)}, bf16[8,512,128]{2,1,0:T(8,128)(2,1)}, f32[8,512,128]{2,0,1:T(8,128)}, bf16[8,1536,128]{2,1,0:T(8,128)(2,1)}, f32[8,512,128]{2,0,1:T...) while((s32[]{:T(128)}, bf16[8,512,128]{2,1,0:T(8,128)(2,1)}, ...), condition=%wide.region_4.6_spmd, body=%wide.region_0.5_spmd.sunk | while | flops 1626930176 | bytes 41177288 | solution.py:139
  358.4 8.0 dynamic_update_slice.37
  366.4 8.0 dynamic_update_slice.38
  392.0 8.0 dynamic_update_slice.37
  400.0 8.0 dynamic_update_slice.38
  425.6 8.0 dynamic_update_slice.37
  433.6 8.0 dynamic_update_slice.38
  459.2 8.0 dynamic_update_slice.37
  467.2 8.0 dynamic_update_slice.38
  492.7 8.0 dynamic_update_slice.37
  500.8 8.0 dynamic_update_slice.38
  526.3 8.0 dynamic_update_slice.37
  534.3 8.0 dynamic_update_slice.38
  559.9 8.0 dynamic_update_slice.37
  567.9 8.0 dynamic_update_slice.38
  593.5 8.0 dynamic_update_slice.37
  650.0 63.4 %all-to-all-done.12 = bf16[32,3,16,8,128]{4,3,2,1,0:T(8,128)(2,1)S(1)} async-done(((bf16[32,3,16,8,128]{4,3,2,1,0:T(8,128)(2,1)}), bf16[32,3,16,8,128]{4,3,2,1,0:T(8,128)(2,1)S(1)}, u32[]{:S(2)}, u32[]{:S(2)}) %all-to-all-start.12) | async-done | bytes 3145760 | tf_op jit(solution)/shard_map/all_to_all | solution.py:163
  737.1 56.2 %all-to-all-done.9 = bf16[32,3,16,8,128]{4,3,2,1,0:T(8,128)(2,1)S(1)} async-done(((bf16[32,3,16,8,128]{4,3,2,1,0:T(8,128)(2,1)}), bf16[32,3,16,8,128]{4,3,2,1,0:T(8,128)(2,1)S(1)}, u32[]{:S(2)}, u32[]{:S(2)}) %all-to-all-start.9) | async-done | bytes 3145760 | tf_op jit(solution)/shard_map/all_to_all | solution.py:160
  810.3 35.1 %all-to-all-done.13 = f32[32,1,16,8,128]{4,3,2,1,0:T(8,128)} async-done(((f32[32,1,16,8,128]{4,3,2,1,0:T(8,128)}), f32[32,1,16,8,128]{4,3,2,1,0:T(8,128)}, u32[]{:S(2)}, u32[]{:S(2)}) %all-to-all-start.13) | async-done | bytes 2097184 | tf_op jit(solution)/shard_map/all_to_all | solution.py:187
  856.8 42.1 %all-to-all-done.10 = f32[32,1,16,8,128]{4,3,2,1,0:T(8,128)S(1)} async-done(((f32[32,1,16,8,128]{4,3,2,1,0:T(8,128)}), f32[32,1,16,8,128]{4,3,2,1,0:T(8,128)S(1)}, u32[]{:S(2)}, u32[]{:S(2)}) %all-to-all-start.10) | async-done | bytes 2097184 | tf_op jit(solution)/shard_map/all_to_all | solution.py:186
  898.8 9.5 %all-to-all-start.14 = ((bf16[8,64,1024]{2,1,0:T(8,128)(2,1)}), bf16[8,64,1024]{2,1,0:T(8,128)(2,1)}, u32[]{:S(2)}, u32[]{:S(2)}) async-start(bf16[8,64,1024]{2,1,0:T(8,128)(2,1)} %all_to_all.142), calls=%async_computation.14 | async-start | bytes 2097152 | tf_op jit(solution)/shard_map/all_to_all | solution.py:198
  911.6 11.9 %all-to-all-done.14 = bf16[8,64,1024]{2,1,0:T(8,128)(2,1)} async-done(((bf16[8,64,1024]{2,1,0:T(8,128)(2,1)}), bf16[8,64,1024]{2,1,0:T(8,128)(2,1)}, u32[]{:S(2)}, u32[]{:S(2)}) %all-to-all-start.14) | async-done | bytes 1048608 | tf_op jit(solution)/shard_map/all_to_all | solution.py:198
  931.2 11.8 %all-to-all-done.11 = bf16[8,64,1024]{2,1,0:T(8,128)(2,1)S(1)} async-done(((bf16[8,64,1024]{2,1,0:T(8,128)(2,1)}), bf16[8,64,1024]{2,1,0:T(8,128)(2,1)S(1)}, u32[]{:S(2)}, u32[]{:S(2)}) %all-to-all-start.11) | async-done | bytes 1048608 | tf_op jit(solution)/shard_map/all_to_all | solution.py:197
  (221 shorter events, 322.7 us)
Async XLA Ops:
  0.6 9.1 copy-start.5
  3.0 21.8 %all-to-all-start = ((bf16[64,8,1024]{2,0,1:T(8,128)(2,1)}), bf16[64,8,1024]{2,0,1:T(8,128)(2,1)S(1)}, u32[]{:S(2)}, u32[]{:S(2)}) async-start(bf16[64,8,1024]{2,0,1:T(8,128)(2,1)} %bitcast.183), calls=%async_computation | async-start | bytes 2097152 | tf_op jit(solution)/shard_map/all_to_all | solution.py:71
  24.8 19.5 %copy-start.1 = (bf16[64,8,1024]{2,0,1:T(8,128)(2,1)}, bf16[64,8,1024]{2,0,1:T(8,128)(2,1)S(1)}, u32[]{:S(2)}) copy-start(bf16[64,8,1024]{2,0,1:T(8,128)(2,1)S(1)} %all-to-all-done) | copy-start | bytes 3145732
  24.8 19.5 %all-to-all-start.1 = ((bf16[64,8,1024]{2,0,1:T(8,128)(2,1)}), bf16[64,8,1024]{2,0,1:T(8,128)(2,1)S(1)}, u32[]{:S(2)}, u32[]{:S(2)}) async-start(bf16[64,8,1024]{2,0,1:T(8,128)(2,1)} %bitcast.182), calls=%async_computation.1 | async-start | bytes 2097152 | tf_op jit(solution)/shard_map/all_to_all | solution.py:72
  44.3 19.5 %all-to-all-start.5 = ((bf16[64,8,1024]{2,0,1:T(8,128)(2,1)}), bf16[64,8,1024]{2,0,1:T(8,128)(2,1)S(1)}, u32[]{:S(2)}, u32[]{:S(2)}) async-start(bf16[64,8,1024]{2,0,1:T(8,128)(2,1)} %bitcast.236), calls=%async_computation.5 | async-start | bytes 2097152 | tf_op jit(solution)/shard_map/all_to_all | solution.py:73
  63.7 42.7 %copy-start.7 = (s32[1,3]{1,0:T(1,128)S(1)}, s32[1,3]{1,0:T(1,128)}, u32[]{:S(2)}) copy-start(s32[1,3]{1,0:T(1,128)} %param.13) | copy-start | bytes 40
  63.7 90.7 %copy-start.6 = (bf16[64,8192]{1,0:T(8,128)(2,1)S(1)}, bf16[64,8192]{1,0:T(8,128)(2,1)}, u32[]{:S(2)}) copy-start(bf16[64,8192]{1,0:T(8,128)(2,1)} %param.12) | copy-start | bytes 3145732
  63.7 36.4 %all-to-all-start.2 = ((bf16[32,1,16,8,128]{4,3,2,1,0:T(8,128)(2,1)}), bf16[32,1,16,8,128]{4,3,2,1,0:T(8,128)(2,1)S(1)}, u32[]{:S(2)}, u32[]{:S(2)}) async-start(bf16[32,1,16,8,128]{4,3,2,1,0:T(8,128)(2,1)} %bitcast.17), calls=%async_computation.2 | async-start | bytes 2097152 | tf_op jit(solution)/shard_map/all_to_all | solution.py:84
  100.2 55.3 %all-to-all-start.6 = ((bf16[32,1,16,8,128]{4,3,2,1,0:T(8,128)(2,1)}), bf16[32,1,16,8,128]{4,3,2,1,0:T(8,128)(2,1)S(1)}, u32[]{:S(2)}, u32[]{:S(2)}) async-start(bf16[32,1,16,8,128]{4,3,2,1,0:T(8,128)(2,1)} %bitcast.30), calls=%async_computation.6 | async-start | bytes 2097152 | tf_op jit(solution)/shard_map/all_to_all | solution.py:91
  155.5 29.4 %all-to-all-start.4 = ((bf16[64,8,1024]{2,0,1:T(8,128)(2,1)}), bf16[64,8,1024]{2,0,1:T(8,128)(2,1)}, u32[]{:S(2)}, u32[]{:S(2)}) async-start(bf16[64,8,1024]{2,0,1:T(8,128)(2,1)} %bitcast.181), calls=%async_computation.4 | async-start | bytes 2097152 | tf_op jit(solution)/shard_map/all_to_all | solution.py:74
  261.2 7.3 copy-start.2
  261.2 76.2 %all-to-all-start.3 = ((bf16[32,3,16,8,128]{4,3,2,1,0:T(8,128)(2,1)}), bf16[32,3,16,8,128]{4,3,2,1,0:T(8,128)(2,1)}, u32[]{:S(2)}, u32[]{:S(2)}) async-start(bf16[32,3,16,8,128]{4,3,2,1,0:T(8,128)(2,1)} %get-tuple-element.240), calls=%async_computation.3 | async-start | bytes 6291456 | tf_op jit(solution)/shard_map/all_to_all | solution.py:105
  613.7 22.2 %all-to-all-start.8 = ((bf16[8,64,1024]{2,1,0:T(8,128)(2,1)}), bf16[8,64,1024]{2,1,0:T(8,128)(2,1)S(1)}, u32[]{:S(2)}, u32[]{:S(2)}) async-start(bf16[8,64,1024]{2,1,0:T(8,128)(2,1)} %all_to_all.130), calls=%async_computation.8 | async-start | bytes 2097152 | tf_op jit(solution)/shard_map/all_to_all | solution.py:196
  636.0 1.0 copy-start.3
  636.9 76.5 %all-to-all-start.12 = ((bf16[32,3,16,8,128]{4,3,2,1,0:T(8,128)(2,1)}), bf16[32,3,16,8,128]{4,3,2,1,0:T(8,128)(2,1)S(1)}, u32[]{:S(2)}, u32[]{:S(2)}) async-start(bf16[32,3,16,8,128]{4,3,2,1,0:T(8,128)(2,1)} %copy.92), calls=%async_computation.12 | async-start | bytes 6291456 | tf_op jit(solution)/shard_map/all_to_all | solution.py:163
  713.4 1.7 copy-start
  715.1 78.3 %all-to-all-start.9 = ((bf16[32,3,16,8,128]{4,3,2,1,0:T(8,128)(2,1)}), bf16[32,3,16,8,128]{4,3,2,1,0:T(8,128)(2,1)S(1)}, u32[]{:S(2)}, u32[]{:S(2)}) async-start(bf16[32,3,16,8,128]{4,3,2,1,0:T(8,128)(2,1)} %copy.86), calls=%async_computation.9 | async-start | bytes 6291456 | tf_op jit(solution)/shard_map/all_to_all | solution.py:160
  793.3 52.1 %all-to-all-start.13 = ((f32[32,1,16,8,128]{4,3,2,1,0:T(8,128)}), f32[32,1,16,8,128]{4,3,2,1,0:T(8,128)}, u32[]{:S(2)}, u32[]{:S(2)}) async-start(f32[32,1,16,8,128]{4,3,2,1,0:T(8,128)} %copy.94), calls=%async_computation.13 | async-start | bytes 4194304 | tf_op jit(solution)/shard_map/all_to_all | solution.py:187
  845.4 53.4 %all-to-all-start.10 = ((f32[32,1,16,8,128]{4,3,2,1,0:T(8,128)}), f32[32,1,16,8,128]{4,3,2,1,0:T(8,128)S(1)}, u32[]{:S(2)}, u32[]{:S(2)}) async-start(f32[32,1,16,8,128]{4,3,2,1,0:T(8,128)} %copy.88), calls=%async_computation.10 | async-start | bytes 4194304 | tf_op jit(solution)/shard_map/all_to_all | solution.py:186
  898.8 24.7 %all-to-all-start.14 = ((bf16[8,64,1024]{2,1,0:T(8,128)(2,1)}), bf16[8,64,1024]{2,1,0:T(8,128)(2,1)}, u32[]{:S(2)}, u32[]{:S(2)}) async-start(bf16[8,64,1024]{2,1,0:T(8,128)(2,1)} %all_to_all.142), calls=%async_computation.14 | async-start | bytes 2097152 | tf_op jit(solution)/shard_map/all_to_all | solution.py:198
  910.3 17.5 %copy-start.4 = (bf16[8,64,1024]{2,1,0:T(8,128)(2,1)S(1)}, bf16[8,64,1024]{2,1,0:T(8,128)(2,1)}, u32[]{:S(2)}) copy-start(bf16[8,64,1024]{2,1,0:T(8,128)(2,1)} %copy-done.3) | copy-start | bytes 3145732
  923.5 19.5 %all-to-all-start.11 = ((bf16[8,64,1024]{2,1,0:T(8,128)(2,1)}), bf16[8,64,1024]{2,1,0:T(8,128)(2,1)S(1)}, u32[]{:S(2)}, u32[]{:S(2)}) async-start(bf16[8,64,1024]{2,1,0:T(8,128)(2,1)} %all_to_all.136), calls=%async_computation.11 | async-start | bytes 2097152 | tf_op jit(solution)/shard_map/all_to_all | solution.py:197
where the time goes:
time: 950 us; the launch traced here: 944 us
  waiting for transfers between devices  354 us (37%)
  local copies, waits for them, and re-layouts  254 us (27%)
  blocking collectives  124 us (13%)
  starting transfers between devices  101 us (11%)
  matrix products  87.2 us (9%)
  other arithmetic  21.5 us (2%)
    dynamic_update_slice x24, local copies, waits for them, and re-layouts, per_device(): lax.map(per_head, (jnp.swapaxes(query_blocks[0], 0, 1), jnp.swapaxes(key_...  137 us
    all_to_all x1, blocking collectives, per_device(): lax.all_to_all(jnp.take(value_table, everyone, axis=0), 'ctx', split_axis...  76.3 us
    all_to_all x1, waiting for transfers between devices, per_device(): lax.all_to_all(to_pieces(value_far, devices, head_groups), 'ctx', split_a...  63.4 us
    all_to_all x1, waiting for transfers between devices, per_device(): lax.all_to_all(to_pieces(key_far, devices, head_groups), 'ctx', split_axi...  56.2 us
    all_to_all x1, waiting for transfers between devices, per_device(): lax.all_to_all(jnp.take(key_table, everyone, axis=0), 'ctx', split_axis=0...  55.4 us
    all_gather x1, blocking collectives, per_device(): everyone = lax.all_gather(chosen, 'ctx', axis=0, tiled=True)  47.8 us
    all_to_all x1, waiting for transfers between devices, per_device(): lax.all_to_all(key_sums.reshape(sum_shape), 'ctx', split_axis=0, concat_a...  42.1 us
    all_to_all x1, waiting for transfers between devices, per_device(): lax.all_to_all(value_sums.reshape(sum_shape), 'ctx', split_axis=0, concat...  35.1 us
  transfers between devices with their start and end apart: 14, of which 13 were waited for; matrix products, arithmetic and copies ran while one was open for 8% of the time, Pallas kernels for 0%

commit v1 on v0

v1 whole, which is shorter than its diff:
```python
import functools

import jax
import jax.numpy as jnp
from jax import lax
from jax.experimental import pallas as pl
from jax.experimental.pallas import tpu as pltpu
from jax.sharding import PartitionSpec as P

H = 64
HD = 128
BLOCK = 512
TOPK = 3
CHUNKS = 4
PIECE = 16
MESH = pl.DeviceIdType.MESH
LOG2E = 1.4426950408889634
masked_score = -1e30


def mm(a, b, dims):
    return lax.dot_general(a, b, (dims, ((), ())), preferred_element_type=jnp.float32)


def kernel(
    nctx,
    nhead,
    q_in,
    k_in,
    v_in,
    g_in,
    chosen_ref,
    q_out,
    k_out,
    v_out,
    kv,
    qg,
    table,
    staging,
    far_grad,
    own_grad,
    parts,
    sums,
    back,
    prev_back,
    done,
    pick,
    unpick,
    score_scr,
    dprob_scr,
    my_list,
    lists,
    list_send,
    list_recv,
    in_send,
    in_recv,
    piece_send,
    piece_recv,
    prev_send,
    prev_recv,
    far_send,
    far_recv,
    grad_send,
    grad_recv,
    pgrad_send,
    pgrad_recv,
    sum_send,
    sum_recv,
    out_send,
    out_recv,
):
    c_me = lax.axis_index("ctx")
    h_me = lax.axis_index("head")
    lanes = kv.shape[-1]
    heads = lanes // HD
    rows = BLOCK // nhead
    group = lanes * CHUNKS
    scaling = HD ** (-0.5)
    factor = scaling * LOG2E
    next_ctx = lax.rem(c_me + 1, nctx)
    last_ctx = lax.rem(c_me + nctx - 1, nctx)

    def ctx_peers(body):
        def step(k, carry):
            body(lax.rem(c_me + k, nctx))
            return carry

        lax.fori_loop(1, nctx, step, 0)

    def head_peers(body):
        def step(k, carry):
            body(lax.rem(h_me + k, nhead))
            return carry

        lax.fori_loop(1, nhead, step, 0)

    def remote(src, dst, send, recv, c_to, h_to):
        return pltpu.make_async_remote_copy(
            src_ref=src,
            dst_ref=dst,
            send_sem=send,
            recv_sem=recv,
            device_id=(c_to, h_to),
            device_id_type=MESH,
        )

    def await_bytes(ref, sem):
        pltpu.make_async_copy(ref, ref, sem).wait()

    barrier = pltpu.get_barrier_semaphore()
    ctx_peers(lambda p: pl.semaphore_signal(barrier, inc=1, device_id=(p, h_me), device_id_type=MESH))
    head_peers(lambda p: pl.semaphore_signal(barrier, inc=1, device_id=(c_me, p), device_id_type=MESH))
    pl.semaphore_wait(barrier, nctx + nhead - 2)

    def slab_columns(peer, c):
        return pl.ds(pl.multiple_of(peer * group + c * lanes, 128), lanes)

    my_rows = pl.ds(pl.multiple_of(h_me * rows, rows), rows)

    def piece_rows(peer):
        return pl.ds(pl.multiple_of(peer * PIECE, PIECE), PIECE)

    def send_in(c, which, src, dst):
        head_peers(
            lambda p: remote(
                src.at[:, slab_columns(p, c)],
                dst.at[my_rows],
                in_send.at[c, which],
                in_recv.at[c, which],
                c_me,
                p,
            ).start()
        )
        pltpu.make_async_copy(
            src.at[:, slab_columns(h_me, c)], dst.at[my_rows], in_recv.at[c, which]
        ).start()

    for c in range(CHUNKS):
        send_in(c, 0, k_in, kv.at[c, 0, 0])
        send_in(c, 0, v_in, kv.at[c, 1, 0])

    lane_slot = lax.rem(lax.broadcasted_iota(jnp.int32, (8, 128), 1) // PIECE, 2)
    first = jnp.where(chosen_ref[0, 1] != c_me, chosen_ref[0, 1], -1)
    second = jnp.where(chosen_ref[0, 2] != c_me, chosen_ref[0, 2], -1)
    my_list[...] = jnp.where(lane_slot == 0, first, second)
    ctx_peers(
        lambda p: remote(my_list, lists.at[c_me], list_send, list_recv, p, h_me).start()
    )
    pltpu.make_async_copy(my_list, lists.at[c_me], list_recv).start()

    for c in range(CHUNKS):
        send_in(c, 1, q_in, qg.at[c, 0])
        send_in(c, 1, g_in, qg.at[c, 1])

    for c in range(CHUNKS):
        await_bytes(kv.at[c, :, 0], in_recv.at[c, 0])
        ctx_peers(
            lambda p: remote(
                kv.at[c, :, 0, piece_rows(p)],
                table.at[c, :, c_me],
                piece_send.at[c],
                piece_recv.at[c],
                p,
                h_me,
            ).start()
        )
        pltpu.make_async_copy(
            kv.at[c, :, 0, piece_rows(c_me)], table.at[c, :, c_me], piece_recv.at[c]
        ).start()
        remote(
            kv.at[c, :, 0], kv.at[c, :, 1], prev_send.at[c], prev_recv.at[c], next_ctx, h_me
        ).start()

    await_bytes(lists, list_recv)
    items = 2 * nctx * PIECE
    keys_total = nctx * PIECE
    width = min(128, items)
    per = width // (2 * PIECE)
    for t in range(items // width):
        lane_owner = lax.broadcasted_iota(jnp.int32, (8, 128), 1) // (2 * PIECE)
        target = lists[t * per]
        for i in range(1, per):
            target = jnp.where(lane_owner == i, lists[t * per + i], target)
        row = lax.broadcasted_iota(jnp.int32, (keys_total, 128), 0)
        lane = lax.broadcasted_iota(jnp.int32, (keys_total, 128), 1)
        hit = (row // PIECE == target[0:1, :]) & (lax.rem(row, PIECE) == lax.rem(lane, PIECE))
        unpick[:, t * width : (t + 1) * width] = jnp.where(hit, 1.0, 0.0).astype(jnp.bfloat16)
        flat = jnp.broadcast_to(target[0:1, :], (128, 128)).astype(jnp.float32).T
        flat = flat.astype(jnp.int32)
        for u in range(max(1, keys_total // 128)):
            wide = min(128, keys_total)
            row = lax.broadcasted_iota(jnp.int32, (128, 128), 0)
            lane = lax.broadcasted_iota(jnp.int32, (128, 128), 1)
            hit = (lane // PIECE + u * (128 // PIECE) == flat) & (
                lax.rem(row, PIECE) == lax.rem(lane, PIECE)
            )
            pick[t * width : (t + 1) * width, u * wide : (u + 1) * wide] = jnp.where(
                hit, 1.0, 0.0
            ).astype(jnp.bfloat16)[:, :wide]

    for c in range(CHUNKS):
        await_bytes(table.at[c], piece_recv.at[c])
        for which in range(2):
            found = mm(pick[...], table[c, which].reshape(keys_total, lanes), ((1,), (0,)))
            staging[c, :, which] = found.astype(jnp.bfloat16).reshape(nctx, 2, PIECE, lanes)
        ctx_peers(
            lambda p: remote(
                staging.at[c, p],
                kv.at[c, :, pl.ds(2, 2), piece_rows(c_me)],
                far_send.at[c],
                far_recv.at[c],
                p,
                h_me,
            ).start()
        )
        pltpu.make_async_copy(
            staging.at[c, c_me], kv.at[c, :, pl.ds(2, 2), piece_rows(c_me)], far_recv.at[c]
        ).start()

    half = BLOCK // 2
    used = [jnp.where(chosen_ref[0, s] != c_me, -(2**20), 2**20) for s in range(TOPK)]

    def tile_offset(t):
        blk = t // 2
        off = jnp.where(blk == 0, t * half, used[2])
        off = jnp.where(blk == 1, used[0], off)
        return jnp.where(blk == 2, used[1], off)

    def folded(x, op):
        return op(x.reshape(half // 8, 8, BLOCK), axis=0)

    for c in range(CHUNKS):
        await_bytes(qg.at[c], in_recv.at[c, 1])
        await_bytes(kv.at[c, :, 1], prev_recv.at[c])
        await_bytes(kv.at[c, :, pl.ds(2, 2)], far_recv.at[c])

        def per_head(n, carry, c=c):
            cols = pl.ds(pl.multiple_of(n * HD, HD), HD)
            q = qg[c, 0, :, cols]
            g = qg[c, 1, :, cols]

            def tile_rows(t):
                return pl.ds(pl.multiple_of(lax.rem(t, 2) * half, half), half)

            def find_scores(t, largest):
                keys = kv[c, 0, t // 2, tile_rows(t), cols]
                s = mm(keys, q, ((1,), (1,)))
                key_at = lax.broadcasted_iota(jnp.int32, (half, BLOCK), 0) + tile_offset(t)
                query_at = lax.broadcasted_iota(jnp.int32, (half, BLOCK), 1)
                s = jnp.where(key_at <= query_at, s, masked_score)
                score_scr[t] = s
                return jnp.maximum(largest, folded(s, jnp.max))

            largest = lax.fori_loop(
                0, 8, find_scores, jnp.full((8, BLOCK), masked_score, jnp.float32)
            )
            largest = jnp.max(largest, axis=0, keepdims=True)

            def find_totals(t, totals):
                values = kv[c, 1, t // 2, tile_rows(t), cols]
                d = mm(values, g, ((1,), (1,)))
                e = jnp.exp2((score_scr[t] - largest) * factor)
                score_scr[t] = e
                dprob_scr[t] = d
                return totals[0] + folded(e, jnp.sum), totals[1] + folded(e * d, jnp.sum)

            zero = jnp.zeros((8, BLOCK), jnp.float32)
            total, total_d = lax.fori_loop(0, 8, find_totals, (zero, zero))
            inverse = 1.0 / jnp.sum(total, axis=0, keepdims=True)
            delta = jnp.sum(total_d, axis=0, keepdims=True) * inverse

            def find_grads(t, dq):
                keys = kv[c, 0, t // 2, tile_rows(t), cols]
                p = score_scr[t] * inverse
                ds = (p * (dprob_scr[t] - delta)).astype(jnp.bfloat16)
                dv = mm(p.astype(jnp.bfloat16), g, ((1,), (0,)))
                dk = mm(ds, q, ((1,), (0,))) * scaling
                return dk, dv, dq + mm(keys, ds, ((0,), (0,)))

            def own_tile(t, dq):
                dk, dv, dq = find_grads(t, dq)
                own_grad[c, 0, tile_rows(t), cols] = dk
                own_grad[c, 1, tile_rows(t), cols] = dv
                return dq

            def far_tile(t, dq):
                dk, dv, dq = find_grads(t, dq)
                far_grad[c, 0, t // 2 - 1, tile_rows(t), cols] = dk.astype(jnp.bfloat16)
                far_grad[c, 1, t // 2 - 1, tile_rows(t), cols] = dv.astype(jnp.bfloat16)
                return dq

            dq = lax.fori_loop(0, 2, own_tile, jnp.zeros((HD, BLOCK), jnp.float32))
            dq = lax.fori_loop(2, 8, far_tile, dq)
            done[c, 0, :, cols] = (dq.T * scaling).astype(jnp.bfloat16)
            return carry

        lax.fori_loop(0, heads, per_head, 0)

        ctx_peers(
            lambda p: remote(
                far_grad.at[c, :, pl.ds(1, 2), piece_rows(p)],
                parts.at[c, :, c_me],
                grad_send.at[c],
                grad_recv.at[c],
                p,
                h_me,
            ).start()
        )
        pltpu.make_async_copy(
            far_grad.at[c, :, pl.ds(1, 2), piece_rows(c_me)], parts.at[c, :, c_me], grad_recv.at[c]
        ).start()
        remote(
            far_grad.at[c, :, 0], prev_back.at[c], pgrad_send.at[c], pgrad_recv.at[c], last_ctx, h_me
        ).start()

    def slab_rows(peer):
        return pl.ds(pl.multiple_of(peer * rows, rows), rows)

    def send_out(c, which, dst):
        head_peers(
            lambda p: remote(
                done.at[c, which, slab_rows(p)],
                dst.at[:, slab_columns(h_me, c)],
                out_send.at[which],
                out_recv.at[which],
                c_me,
                p,
            ).start()
        )
        pltpu.make_async_copy(
            done.at[c, which, my_rows], dst.at[:, slab_columns(h_me, c)], out_recv.at[which]
        ).start()

    for c in range(CHUNKS):
        await_bytes(parts.at[c], grad_recv.at[c])
        for which in range(2):
            total = mm(unpick[...], parts[c, which].reshape(items, lanes), ((1,), (0,)))
            sums[c, :, which] = total.astype(jnp.bfloat16).reshape(nctx, PIECE, lanes)
        ctx_peers(
            lambda p: remote(
                sums.at[c, p],
                back.at[c, :, piece_rows(c_me)],
                sum_send.at[c],
                sum_recv.at[c],
                p,
                h_me,
            ).start()
        )
        pltpu.make_async_copy(
            sums.at[c, c_me], back.at[c, :, piece_rows(c_me)], sum_recv.at[c]
        ).start()
        send_out(c, 0, q_out)

    for c in range(CHUNKS):
        await_bytes(prev_back.at[c], pgrad_recv.at[c])
        await_bytes(back.at[c], sum_recv.at[c])
        for which in range(2):
            total = own_grad[c, which] + prev_back[c, which].astype(jnp.float32)
            total = total + back[c, which].astype(jnp.float32)
            done[c, 1 + which] = total.astype(jnp.bfloat16)
        send_out(c, 1, k_out)
        send_out(c, 2, v_out)

    others = pl.ds(0, nctx - 1)
    other_rows = pl.ds(0, (nctx - 1) * PIECE)
    slab_others = pl.ds(0, (nhead - 1) * rows)
    await_bytes(lists.at[others], list_send)
    for c in range(CHUNKS):
        await_bytes(kv.at[c, :, 0, slab_others], in_send.at[c, 0])
        await_bytes(qg.at[c, :, slab_others], in_send.at[c, 1])
        await_bytes(kv.at[c, :, 0, other_rows], piece_send.at[c])
        await_bytes(kv.at[c, :, 0], prev_send.at[c])
        await_bytes(staging.at[c, others], far_send.at[c])
        await_bytes(far_grad.at[c, :, pl.ds(1, 2), other_rows], grad_send.at[c])
        await_bytes(far_grad.at[c, :, 0], pgrad_send.at[c])
        await_bytes(sums.at[c, others], sum_send.at[c])
    for which, out in enumerate((q_out, k_out, v_out)):
        await_bytes(done.at[:, which, slab_others], out_send.at[which])
        await_bytes(out, out_recv.at[which])


def per_device(queries, key_vectors, value_vectors, out_grad, chosen):
    nctx = lax.axis_size("ctx")
    nhead = lax.axis_size("head")
    lanes = H * HD // nhead // CHUNKS
    n = CHUNKS
    bf = jnp.bfloat16
    f32 = jnp.float32
    dma = pltpu.SemaphoreType.DMA
    anywhere = pl.BlockSpec(memory_space=pl.ANY)
    slab = jax.ShapeDtypeStruct(queries.shape, bf)
    scratch = [
        pltpu.VMEM((n, 2, 4, BLOCK, lanes), bf),
        pltpu.VMEM((n, 2, BLOCK, lanes), bf),
        pltpu.VMEM((n, 2, nctx, PIECE, lanes), bf),
        pltpu.VMEM((n, nctx, 2, 2, PIECE, lanes), bf),
        pltpu.VMEM((n, 2, 3, BLOCK, lanes), bf),
        pltpu.VMEM((n, 2, BLOCK, lanes), f32),
        pltpu.VMEM((n, 2, nctx, 2, PIECE, lanes), bf),
        pltpu.VMEM((n, nctx, 2, PIECE, lanes), bf),
        pltpu.VMEM((n, 2, BLOCK, lanes), bf),
        pltpu.VMEM((n, 2, BLOCK, lanes), bf),
        pltpu.VMEM((n, 3, BLOCK, lanes), bf),
        pltpu.VMEM((2 * nctx * PIECE, nctx * PIECE), bf),
        pltpu.VMEM((nctx * PIECE, 2 * nctx * PIECE), bf),
        pltpu.VMEM((8, BLOCK // 2, BLOCK), f32),
        pltpu.VMEM((8, BLOCK // 2, BLOCK), f32),
        pltpu.VMEM((8, 128), jnp.int32),
        pltpu.VMEM((nctx, 8, 128), jnp.int32),
        dma,
        dma,
        dma((n, 2)),
        dma((n, 2)),
    ]
    scratch += [dma((n,)) for _ in range(12)]
    scratch += [dma((3,)), dma((3,))]
    return pl.pallas_call(
        functools.partial(kernel, nctx, nhead),
        out_shape=(slab, slab, slab),
        in_specs=[anywhere] * 4 + [pl.BlockSpec(memory_space=pltpu.SMEM)],
        out_specs=(anywhere,) * 3,
        scratch_shapes=scratch,
        compiler_params=pltpu.CompilerParams(
            collective_id=0, has_side_effects=True, vmem_limit_bytes=60 * 2**20
        ),
        name="sparse_attention_backward",
    )(queries, key_vectors, value_vectors, out_grad, chosen)


def solution(mesh):
    slabs = P(("ctx", "head"), None)
    return jax.shard_map(
        per_device,
        mesh=mesh,
        in_specs=(slabs, slabs, slabs, slabs, P("ctx", None)),
        out_specs=(slabs, slabs, slabs),
        check_vma=False,
    )
```

time: 950 us -> 386 us (0.41)
  Pallas kernels: 0 us -> 381 us
  waiting for transfers between devices: 354 us -> 0 us
  local copies, waits for them, and re-layouts: 254 us -> 4.93 us
  blocking collectives: 124 us -> 0 us
  starting transfers between devices: 101 us -> 0 us
  matrix products: 87.2 us -> 0 us
  other arithmetic: 21.5 us -> 0 us
    pallas_call x0 -> x1, Pallas kernels: none -> 381 us  [per_device(): pl.pallas_call(functools.partial(kernel, nctx, nhead), out_shape=(slab, s...]
    all_to_all x14 -> x0, waiting for transfers between devices: 354 us -> none  [the longest x1 63.4 us: per_device(): lax.all_to_all(to_pieces(value_far, devices, head_groups), 'ctx', split_a...]
    dynamic_update_slice x24 -> x0, local copies, waits for them, and re-layouts: 137 us -> none  [per_device(): lax.map(per_head, (jnp.swapaxes(query_blocks[0], 0, 1), jnp.swapaxes(key_...]
    all_to_all x14 -> x0, starting transfers between devices: 101 us -> none  [the longest x1 14.2 us: per_device(): lax.all_to_all(out_grad, 'head', split_axis=1, concat_axis=0, tiled=True)]
    dot_general x50 -> x0, matrix products: 87.2 us -> none  [the longest x8 16.6 us: head_terms(): jnp.dot(grad_rows, value_rows.T, preferred_element_type=jnp.float32)]
    all_to_all x1 -> x0, blocking collectives: 76.3 us -> none  [per_device(): lax.all_to_all(jnp.take(value_table, everyone, axis=0), 'ctx', split_axis...]
    all_gather x1 -> x0, blocking collectives: 47.8 us -> none  [per_device(): everyone = lax.all_gather(chosen, 'ctx', axis=0, tiled=True)]
    squeeze x32 -> x0, local copies, waits for them, and re-layouts: 31.1 us -> none  [per_device(): lax.map(per_head, (jnp.swapaxes(query_blocks[0], 0, 1), jnp.swapaxes(key_...]
  transfers between devices with their start and end apart: 14 -> 0, of which waited for: 13 -> 0; matrix products, arithmetic and copies ran while one was open for 8% -> 0% of each run, Pallas kernels for 0% -> 0%
where the time goes in v1:
time: 386 us
  Pallas kernels  381 us (99%)
  local copies, waits for them, and re-layouts  4.93 us (1%)
    pallas_call x1, Pallas kernels, per_device(): pl.pallas_call(functools.partial(kernel, nctx, nhead), out_shape=(slab, s...  381 us

profile of v1, /device:TPU:1, one launch (start us, length us, event | category | flops | bytes accessed | tf_op | source)
XLA Modules:
  0.0 386.1 jit_solution(13632096437354970902)
XLA Ops:
  0.6 380.5 %sparse_attention_backward.1 = (bf16[64,8192]{1,0:T(8,128)(2,1)}, bf16[64,8192]{1,0:T(8,128)(2,1)}, bf16[64,8192]{1,0:T(8,128)(2,1)}) custom-call(bf16[64,8192]{1,0:T(8,128)(2,1)} %q_in.1, bf16[64,8192]{1,0:T(8,128)(2,1)} %k_in.1, bf16[64,8192]{1,0:T(8,128)(2,1)} %v_in.1, bf16[64,8192]{1,0:T(8,128)(2,1)} %g_in.1, s32[1,3]{1,0:T(1,128)} %chosen_ref.1), custom_call_target="tpu_custom_call" | custom-call | tf_op jit(solution)/shard_map/sparse_attention_backward/pallas_call | solution.py:417
  381.2 0.0 copy-start.1
  381.2 2.4 copy.11
  383.5 0.0 copy-done.1
  383.5 0.0 copy-start
  383.5 1.0 copy.12
  384.5 0.6 copy-done
  385.1 1.0 copy.13
Async XLA Ops:
  381.2 2.4 copy-start.1
  383.5 1.6 copy-start

commit v2 on v0

v2 whole, which is shorter than its diff:
```python
import functools

import jax
import jax.numpy as jnp
from jax import lax
from jax.experimental import pallas as pl
from jax.experimental.pallas import tpu as pltpu
from jax.sharding import PartitionSpec as P

H = 64
HD = 128
BLOCK = 512
TOPK = 3
RING = 4
PIECE = 16
MESH = pl.DeviceIdType.MESH
LOG2E = 1.4426950408889634
masked_score = -1e30
KEY, VALUE = 0, 1
QUERY, GRAD = 0, 1


def mm(a, b, dims):
    return lax.dot_general(a, b, (dims, ((), ())), preferred_element_type=jnp.float32)


def kernel(
    levels,
    nhead,
    q_in,
    k_in,
    v_in,
    g_in,
    chosen_ref,
    q_out,
    k_out,
    v_out,
    keys,
    values,
    qg,
    weights,
    scratch,
    pairs,
    own,
    partial,
    halves,
    parts,
    done,
    choose,
    my_list,
    lists,
    targets,
    list_send,
    list_recv,
    list_local,
    in_send,
    in_recv,
    ring_send,
    ring_recv,
    part_send,
    part_recv,
    out_send,
    out_recv,
):
    c_me = lax.axis_index("ctx")
    h_me = lax.axis_index("head")
    z_me = c_me // RING
    x_me = lax.rem(c_me, RING)
    rows = BLOCK // nhead
    column_chunks = nhead // 2
    chunk = BLOCK // column_chunks
    half = BLOCK // 2
    scaling = HD ** (-0.5)
    factor = scaling * LOG2E
    group = levels * nhead

    def remote(src, dst, send, recv, z_to, x_to, h_to):
        return pltpu.make_async_remote_copy(
            src_ref=src,
            dst_ref=dst,
            send_sem=send,
            recv_sem=recv,
            device_id=(z_to * RING + x_to, h_to),
            device_id_type=MESH,
        )

    def await_bytes(ref, sem):
        pltpu.make_async_copy(ref, ref, sem).wait()

    def group_peers(body):
        def step(k, carry):
            body(lax.rem(z_me + lax.rem(k, levels), levels), lax.rem(h_me + k // levels, nhead))
            return carry

        lax.fori_loop(1, group, step, 0)

    def signal(z_to, x_to, h_to):
        pl.semaphore_signal(
            barrier, inc=1, device_id=(z_to * RING + x_to, h_to), device_id_type=MESH
        )

    barrier = pltpu.get_barrier_semaphore()
    group_peers(lambda z, h: signal(z, x_me, h))
    for x in (lax.rem(x_me + 1, RING), lax.rem(x_me + RING - 1, RING)):
        signal(z_me, x, h_me)
    pl.semaphore_wait(barrier, group + 1)

    def head_columns(z, h):
        return pl.ds(pl.multiple_of((z * nhead + h) * HD, HD), HD)

    def slab_rows(h):
        return pl.ds(pl.multiple_of(h * rows, rows), rows)

    def send_in(which, src, dst):
        group_peers(
            lambda z, h: remote(
                src.at[:, head_columns(z, h)],
                dst.at[z_me, slab_rows(h_me)],
                in_send.at[which],
                in_recv.at[which],
                z,
                x_me,
                h,
            ).start()
        )
        pltpu.make_async_copy(
            src.at[:, head_columns(z_me, h_me)], dst.at[z_me, slab_rows(h_me)], in_recv.at[which]
        ).start()

    send_in(0, k_in, keys.at[x_me])

    lane = lax.broadcasted_iota(jnp.int32, (8, 128), 1)
    my_list[...] = jnp.where(
        lane == 0, chosen_ref[0, 0], jnp.where(lane == 1, chosen_ref[0, 1], chosen_ref[0, 2])
    )

    def send_list(k, carry):
        remote(
            my_list, lists.at[z_me], list_send, list_recv, lax.rem(z_me + k, levels), x_me, h_me
        ).start()
        return carry

    lax.fori_loop(1, levels, send_list, 0)
    pltpu.make_async_copy(my_list, lists.at[z_me], list_recv).start()

    send_in(1, q_in, qg.at[QUERY])
    send_in(2, v_in, values.at[x_me])
    send_in(3, g_in, qg.at[GRAD])

    await_bytes(lists, list_recv)
    to_scalars = pltpu.make_async_copy(lists, targets, list_local)
    to_scalars.start()
    to_scalars.wait()

    span = levels * PIECE
    for s in range(TOPK):
        lane = lax.broadcasted_iota(jnp.int32, (RING * span, span), 1)
        row = lax.broadcasted_iota(jnp.int32, (RING * span, span), 0)
        target = jnp.full((RING * span, span), -1, jnp.int32)
        for z in range(levels):
            target = jnp.where(lane // PIECE == z, targets[z, 0, s], target)
        block = lax.rem(row // PIECE, levels) * RING + row // span
        hit = (block == target) & (lax.rem(row, PIECE) == lax.rem(lane, PIECE))
        choose[:, s * span : (s + 1) * span] = jnp.where(hit, 1.0, 0.0).astype(jnp.bfloat16)

    right = lax.rem(x_me + 1, RING)
    left = lax.rem(x_me + RING - 1, RING)
    low = pl.ds(0, levels // 2)
    high = pl.ds(levels // 2, levels // 2)

    def ring_copy(src, dst, sems, to):
        return remote(src, dst, sems[0], sems[1], z_me, to, h_me)

    def share(which, arrived, blocks):
        await_bytes(blocks.at[x_me], in_recv.at[arrived])
        for side, to in enumerate((right, left)):
            ring_copy(
                blocks.at[x_me],
                blocks.at[x_me],
                (ring_send.at[which, side], ring_recv.at[which, side]),
                to,
            ).start()

    def pass_on(which, blocks):
        for side, (source, part, to) in enumerate(((left, low, right), (right, high, left))):
            await_bytes(blocks.at[source], ring_recv.at[which, side])
            ring_copy(
                blocks.at[source, part],
                blocks.at[source, part],
                (ring_send.at[which, 2 + side], ring_recv.at[which, 2 + side]),
                to,
            ).start()

    def await_shared(which, blocks):
        for side, part in enumerate((low, high)):
            await_bytes(blocks.at[0, part], ring_recv.at[which, 2 + side])

    def tile_rows(t):
        return pl.ds(pl.multiple_of(lax.rem(t, 2) * half, half), half)

    def tile_block(z, t):
        mine = z * RING + x_me
        block = jnp.where(t < 2, mine, targets[z, 0, jnp.maximum(t // 2 - 1, 0)])
        far = jnp.where(block != mine, -(2**20), 2**20)
        return lax.rem(block, RING), block // RING, jnp.where(t < 2, t * half, far)

    def folded(x, op):
        return op(x.reshape(half // 8, 8, BLOCK), axis=0)

    def level_loop(body, start=0, stop=levels):
        def step(k, carry):
            body(lax.rem(z_me + k, levels))
            return carry

        lax.fori_loop(start, stop, step, 0)

    share(KEY, 0, keys)
    pass_on(KEY, keys)
    await_bytes(qg.at[QUERY], in_recv.at[1])
    await_shared(KEY, keys)

    def find_weights(z):
        q = qg[QUERY, z]

        def find_scores(t, largest):
            xb, zb, offset = tile_block(z, t)
            s = mm(keys[xb, zb, tile_rows(t)], q, ((1,), (1,)))
            key_at = lax.broadcasted_iota(jnp.int32, (half, BLOCK), 0) + offset
            query_at = lax.broadcasted_iota(jnp.int32, (half, BLOCK), 1)
            s = jnp.where(key_at <= query_at, s, masked_score)
            scratch[t] = s
            return jnp.maximum(largest, folded(s, jnp.max))

        largest = lax.fori_loop(
            0, 8, find_scores, jnp.full((8, BLOCK), masked_score, jnp.float32)
        )
        largest = jnp.max(largest, axis=0, keepdims=True)

        def find_total(t, total):
            e = jnp.exp2((scratch[t] - largest) * factor)
            scratch[t] = e
            return total + folded(e, jnp.sum)

        total = lax.fori_loop(0, 8, find_total, jnp.zeros((8, BLOCK), jnp.float32))
        inverse = 1.0 / jnp.sum(total, axis=0, keepdims=True)

        def divide(t, carry):
            weights[z, t] = (scratch[t] * inverse).astype(jnp.bfloat16)
            return carry

        lax.fori_loop(0, 8, divide, 0)

    level_loop(find_weights, 0, levels // 2)
    share(VALUE, 2, values)
    level_loop(find_weights, levels // 2, levels)

    pass_on(VALUE, values)
    await_bytes(qg.at[GRAD], in_recv.at[3])

    def find_value_terms(z):
        g = qg[GRAD, z]

        def own_tile(t, carry):
            own[VALUE, z, tile_rows(t)] = mm(weights[z, t], g, ((1,), (0,)))
            return carry

        def far_tile(t, carry):
            term = mm(weights[z, t], g, ((1,), (0,)))
            pairs[VALUE, t // 2 - 1, z, tile_rows(t)] = term.astype(jnp.bfloat16)
            return carry

        lax.fori_loop(0, 2, own_tile, 0)
        lax.fori_loop(2, 8, far_tile, 0)

    level_loop(find_value_terms)

    y_me = h_me // 2

    across = lax.rem(x_me + 2, RING)

    def chunk_start(i):
        return lax.rem(y_me + i, column_chunks) * chunk

    def chunk_rows(i):
        return pl.ds(pl.multiple_of(chunk_start(i), chunk), chunk)

    def send_terms(which):
        for i in range(column_chunks):

            def add_rows(n, carry, i=i):
                at = pl.ds(pl.multiple_of(chunk_start(i) + n * PIECE, PIECE), PIECE)
                terms = pairs[which, :, :, at].reshape(TOPK * span, HD)
                total = mm(choose[...], terms, ((1,), (0,)))
                partial[which, :, :, at] = total.astype(jnp.bfloat16).reshape(
                    RING, levels, PIECE, HD
                )
                return carry

            lax.fori_loop(0, chunk // PIECE, add_rows, 0)
            at = chunk_rows(i)
            for side, (part, to) in enumerate(((low, right), (high, left))):
                ring_copy(
                    partial.at[which, across, part, at],
                    halves.at[which, side, :, at],
                    (part_send.at[which, side, i], part_recv.at[which, side, i]),
                    to,
                ).start()

    def send_sums(which):
        for i in range(column_chunks):
            at = chunk_rows(i)
            for side, (start, to) in enumerate(((0, right), (levels // 2, left))):
                await_bytes(halves.at[which, side, :, at], part_recv.at[which, side, i])

                def add_level(n, carry, at=at, side=side, start=start, to=to):
                    both = partial[which, to, start + n, at].astype(jnp.float32)
                    both = both + halves[which, side, n, at].astype(jnp.float32)
                    partial[which, to, start + n, at] = both.astype(jnp.bfloat16)
                    return carry

                lax.fori_loop(0, levels // 2, add_level, 0)
                ring_copy(
                    partial.at[which, to, :, at],
                    parts.at[which, side, :, at],
                    (part_send.at[which, 2 + side, i], part_recv.at[which, 2 + side, i]),
                    to,
                ).start()

    def send_out(which, z, h, dst):
        here = done.at[which, z, slab_rows(h)]
        there = dst.at[:, head_columns(z_me, h_me)]
        mine = (z == z_me) & (h == h_me)

        @pl.when(mine)
        def _():
            pltpu.make_async_copy(here, there, out_recv.at[which]).start()

        @pl.when(jnp.logical_not(mine))
        def _():
            remote(here, there, out_send.at[which], out_recv.at[which], z, x_me, h).start()

    def finish(which, dst):
        for i in range(column_chunks):
            at = chunk_rows(i)
            for side in range(2):
                await_bytes(parts.at[which, side, :, at], part_recv.at[which, 2 + side, i])

            def add_level(z, at=at):
                total = own[which, z, at] + partial[which, x_me, z, at].astype(jnp.float32)
                for side in range(2):
                    total = total + parts[which, side, z, at].astype(jnp.float32)
                done[1 + which, z, at] = total.astype(jnp.bfloat16)

            level_loop(add_level)

            def send_level(z, i=i):
                for n in range(2):
                    send_out(1 + which, z, lax.rem(y_me + i, column_chunks) * 2 + n, dst)

            level_loop(send_level)

    send_terms(VALUE)

    await_shared(VALUE, values)

    def find_key_terms(z):
        q = qg[QUERY, z]
        g = qg[GRAD, z]

        def find_dprobs(t, delta):
            xb, zb, offset = tile_block(z, t)
            d = mm(values[xb, zb, tile_rows(t)], g, ((1,), (1,)))
            scratch[t] = d
            return delta + folded(weights[z, t].astype(jnp.float32) * d, jnp.sum)

        delta = lax.fori_loop(0, 8, find_dprobs, jnp.zeros((8, BLOCK), jnp.float32))
        delta = jnp.sum(delta, axis=0, keepdims=True)

        def find_terms(t, dq):
            xb, zb, offset = tile_block(z, t)
            key_rows = keys[xb, zb, tile_rows(t)]
            ds = (weights[z, t].astype(jnp.float32) * (scratch[t] - delta)).astype(jnp.bfloat16)
            return mm(ds, q, ((1,), (0,))) * scaling, dq + mm(key_rows, ds, ((0,), (0,)))

        def own_tile(t, dq):
            dk, dq = find_terms(t, dq)
            own[KEY, z, tile_rows(t)] = dk
            return dq

        def far_tile(t, dq):
            dk, dq = find_terms(t, dq)
            pairs[KEY, t // 2 - 1, z, tile_rows(t)] = dk.astype(jnp.bfloat16)
            return dq

        dq = lax.fori_loop(0, 2, own_tile, jnp.zeros((HD, BLOCK), jnp.float32))
        dq = lax.fori_loop(2, 8, far_tile, dq)
        done[0, z] = (dq.T * scaling).astype(jnp.bfloat16)

        def send_rows(k, carry):
            send_out(0, z, lax.rem(h_me + k, nhead), q_out)
            return carry

        lax.fori_loop(0, nhead, send_rows, 0)

    level_loop(find_key_terms, 0, levels // 2)
    send_sums(VALUE)
    level_loop(find_key_terms, levels // 2, levels)
    send_terms(KEY)
    send_sums(KEY)
    finish(VALUE, v_out)
    finish(KEY, k_out)

    others_columns = pl.ds(0, (group - 1) * HD)
    await_bytes(lists.at[pl.ds(0, levels - 1)], list_send)
    for which, src in enumerate((k_in, q_in, v_in, g_in)):
        await_bytes(src.at[:, others_columns], in_send.at[which])
    for which in range(2):
        for side in range(2):
            await_bytes(keys.at[0], ring_send.at[which, side])
            await_bytes(keys.at[0, low], ring_send.at[which, 2 + side])
            for i in range(column_chunks):
                at = pl.ds(0, chunk)
                await_bytes(halves.at[which, side, :, at], part_send.at[which, side, i])
                await_bytes(parts.at[which, side, :, at], part_send.at[which, 2 + side, i])
    for which, out in enumerate((q_out, k_out, v_out)):
        await_bytes(out.at[:, others_columns], out_send.at[which])
        await_bytes(out, out_recv.at[which])


def per_device(queries, key_vectors, value_vectors, out_grad, chosen):
    levels = lax.axis_size("ctx") // RING
    nhead = lax.axis_size("head")
    bf = jnp.bfloat16
    f32 = jnp.float32
    dma = pltpu.SemaphoreType.DMA
    anywhere = pl.BlockSpec(memory_space=pl.ANY)
    slab = jax.ShapeDtypeStruct(queries.shape, bf)
    span = levels * PIECE
    scratch = [
        pltpu.VMEM((RING, levels, BLOCK, HD), bf),
        pltpu.VMEM((RING, levels, BLOCK, HD), bf),
        pltpu.VMEM((2, levels, BLOCK, HD), bf),
        pltpu.VMEM((levels, 8, BLOCK // 2, BLOCK), bf),
        pltpu.VMEM((8, BLOCK // 2, BLOCK), f32),
        pltpu.VMEM((2, TOPK, levels, BLOCK, HD), bf),
        pltpu.VMEM((2, levels, BLOCK, HD), f32),
        pltpu.VMEM((2, RING, levels, BLOCK, HD), bf),
        pltpu.VMEM((2, 2, levels // 2, BLOCK, HD), bf),
        pltpu.VMEM((2, 2, levels, BLOCK, HD), bf),
        pltpu.VMEM((3, levels, BLOCK, HD), bf),
        pltpu.VMEM((RING * span, TOPK * span), bf),
        pltpu.VMEM((8, 128), jnp.int32),
        pltpu.VMEM((levels, 8, 128), jnp.int32),
        pltpu.SMEM((levels, 8, 128), jnp.int32),
        dma,
        dma,
        dma,
        dma((4,)),
        dma((4,)),
        dma((2, 4)),
        dma((2, 4)),
        dma((2, 4, nhead // 2)),
        dma((2, 4, nhead // 2)),
        dma((3,)),
        dma((3,)),
    ]
    return pl.pallas_call(
        functools.partial(kernel, levels, nhead),
        out_shape=(slab, slab, slab),
        in_specs=[anywhere] * 4 + [pl.BlockSpec(memory_space=pltpu.SMEM)],
        out_specs=(anywhere,) * 3,
        scratch_shapes=scratch,
        compiler_params=pltpu.CompilerParams(
            collective_id=0, has_side_effects=True, vmem_limit_bytes=62 * 2**20
        ),
        name="sparse_attention_backward",
    )(queries, key_vectors, value_vectors, out_grad, chosen)


def solution(mesh):
    slabs = P(("ctx", "head"), None)
    return jax.shard_map(
        per_device,
        mesh=mesh,
        in_specs=(slabs, slabs, slabs, slabs, P("ctx", None)),
        out_specs=(slabs, slabs, slabs),
        check_vma=False,
    )
```

time: 950 us -> 238 us (0.25)
  waiting for transfers between devices: 354 us -> 0 us
  local copies, waits for them, and re-layouts: 254 us -> 4.93 us
  Pallas kernels: 0 us -> 232 us
  blocking collectives: 124 us -> 0 us
  starting transfers between devices: 101 us -> 0 us
  matrix products: 87.2 us -> 0 us
  other arithmetic: 21.5 us -> 0 us
    all_to_all x14 -> x0, waiting for transfers between devices: 354 us -> none  [the longest x1 63.4 us: per_device(): lax.all_to_all(to_pieces(value_far, devices, head_groups), 'ctx', split_a...]
    pallas_call x0 -> x1, Pallas kernels: none -> 232 us  [per_device(): pl.pallas_call(functools.partial(kernel, levels, nhead), out_shape=(slab,...]
    dynamic_update_slice x24 -> x0, local copies, waits for them, and re-layouts: 137 us -> none  [per_device(): lax.map(per_head, (jnp.swapaxes(query_blocks[0], 0, 1), jnp.swapaxes(key_...]
    all_to_all x14 -> x0, starting transfers between devices: 101 us -> none  [the longest x1 14.2 us: per_device(): lax.all_to_all(out_grad, 'head', split_axis=1, concat_axis=0, tiled=True)]
    dot_general x50 -> x0, matrix products: 87.2 us -> none  [the longest x8 16.6 us: head_terms(): jnp.dot(grad_rows, value_rows.T, preferred_element_type=jnp.float32)]
    all_to_all x1 -> x0, blocking collectives: 76.3 us -> none  [per_device(): lax.all_to_all(jnp.take(value_table, everyone, axis=0), 'ctx', split_axis...]
    all_gather x1 -> x0, blocking collectives: 47.8 us -> none  [per_device(): everyone = lax.all_gather(chosen, 'ctx', axis=0, tiled=True)]
    squeeze x32 -> x0, local copies, waits for them, and re-layouts: 31.1 us -> none  [per_device(): lax.map(per_head, (jnp.swapaxes(query_blocks[0], 0, 1), jnp.swapaxes(key_...]
  transfers between devices with their start and end apart: 14 -> 0, of which waited for: 13 -> 0; matrix products, arithmetic and copies ran while one was open for 8% -> 0% of each run, Pallas kernels for 0% -> 0%
where the time goes in v2:
time: 238 us
  Pallas kernels  232 us (97%)
  local copies, waits for them, and re-layouts  4.93 us (2%)
    pallas_call x1, Pallas kernels, per_device(): pl.pallas_call(functools.partial(kernel, levels, nhead), out_shape=(slab,...  232 us
    unnamed x7, local copies, waits for them, and re-layouts  4.93 us

profile of v2, /device:TPU:1, one launch (start us, length us, event | category | flops | bytes accessed | tf_op | source)
XLA Modules:
  0.0 237.7 jit_solution(12965647755902070203)
XLA Ops:
  0.6 232.1 %sparse_attention_backward.1 = (bf16[64,8192]{1,0:T(8,128)(2,1)}, bf16[64,8192]{1,0:T(8,128)(2,1)}, bf16[64,8192]{1,0:T(8,128)(2,1)}) custom-call(bf16[64,8192]{1,0:T(8,128)(2,1)} %q_in.1, bf16[64,8192]{1,0:T(8,128)(2,1)} %k_in.1, bf16[64,8192]{1,0:T(8,128)(2,1)} %v_in.1, bf16[64,8192]{1,0:T(8,128)(2,1)} %g_in.1, s32[1,3]{1,0:T(1,128)} %chosen_ref.1), custom_call_target="tpu_custom_call" | custom-call | tf_op jit(solution)/shard_map/sparse_attention_backward/pallas_call | solution.py:467
  232.8 0.0 copy-start.1
  232.8 2.4 copy.11
  235.1 0.0 copy-done.1
  235.1 0.0 copy-start
  235.1 1.0 copy.12
  236.1 0.6 copy-done
  236.7 1.0 copy.13
Async XLA Ops:
  232.8 2.4 copy-start.1
  235.1 1.6 copy-start

commit v3 on v2

--- a/solution.py
+++ b/solution.py
@@ -87,9 +87,20 @@
     def await_bytes(ref, sem):
         pltpu.make_async_copy(ref, ref, sem).wait()
 
+    def near_level(k):
+        step = jnp.where(lax.rem(k, 2) == 1, (k + 1) // 2, levels - k // 2)
+        return lax.rem(z_me + step, levels)
+
     def group_peers(body):
         def step(k, carry):
             body(lax.rem(z_me + lax.rem(k, levels), levels), lax.rem(h_me + k // levels, nhead))
+            return carry
+
+        lax.fori_loop(1, group, step, 0)
+
+    def near_peers_first(body):
+        def step(k, carry):
+            body(near_level(k // nhead), lax.rem(h_me + lax.rem(k, nhead), nhead))
             return carry
 
         lax.fori_loop(1, group, step, 0)
@@ -111,23 +122,25 @@
     def slab_rows(h):
         return pl.ds(pl.multiple_of(h * rows, rows), rows)
 
-    def send_in(which, src, dst):
-        group_peers(
+    def send_in(which, src, dst, peers):
+        peers(
             lambda z, h: remote(
                 src.at[:, head_columns(z, h)],
                 dst.at[z_me, slab_rows(h_me)],
                 in_send.at[which],
-                in_recv.at[which],
+                in_recv.at[which, z_me],
                 z,
                 x_me,
                 h,
             ).start()
         )
         pltpu.make_async_copy(
-            src.at[:, head_columns(z_me, h_me)], dst.at[z_me, slab_rows(h_me)], in_recv.at[which]
+            src.at[:, head_columns(z_me, h_me)],
+            dst.at[z_me, slab_rows(h_me)],
+            in_recv.at[which, z_me],
         ).start()
 
-    send_in(0, k_in, keys.at[x_me])
+    send_in(0, k_in, keys.at[x_me], group_peers)
 
     lane = lax.broadcasted_iota(jnp.int32, (8, 128), 1)
     my_list[...] = jnp.where(
@@ -143,9 +156,9 @@
     lax.fori_loop(1, levels, send_list, 0)
     pltpu.make_async_copy(my_list, lists.at[z_me], list_recv).start()
 
-    send_in(1, q_in, qg.at[QUERY])
-    send_in(2, v_in, values.at[x_me])
-    send_in(3, g_in, qg.at[GRAD])
+    send_in(1, v_in, values.at[x_me], group_peers)
+    send_in(2, q_in, qg.at[QUERY], near_peers_first)
+    send_in(3, g_in, qg.at[GRAD], near_peers_first)
 
     await_bytes(lists, list_recv)
     to_scalars = pltpu.make_async_copy(lists, targets, list_local)
@@ -171,8 +184,12 @@
     def ring_copy(src, dst, sems, to):
         return remote(src, dst, sems[0], sems[1], z_me, to, h_me)
 
-    def share(which, arrived, blocks):
-        await_bytes(blocks.at[x_me], in_recv.at[arrived])
+    def share(which, blocks):
+        def await_level(z, carry):
+            await_bytes(blocks.at[x_me, z], in_recv.at[which, z])
+            return carry
+
+        lax.fori_loop(0, levels, await_level, 0)
         for side, to in enumerate((right, left)):
             ring_copy(
                 blocks.at[x_me],
@@ -209,17 +226,18 @@
 
     def level_loop(body, start=0, stop=levels):
         def step(k, carry):
-            body(lax.rem(z_me + k, levels))
+            body(near_level(k))
             return carry
 
         lax.fori_loop(start, stop, step, 0)
 
-    share(KEY, 0, keys)
+    share(KEY, keys)
     pass_on(KEY, keys)
-    await_bytes(qg.at[QUERY], in_recv.at[1])
+    share(VALUE, values)
     await_shared(KEY, keys)
 
     def find_weights(z):
+        await_bytes(qg.at[QUERY, z], in_recv.at[2, z])
         q = qg[QUERY, z]
 
         def find_scores(t, largest):
@@ -232,7 +250,7 @@
             return jnp.maximum(largest, folded(s, jnp.max))
 
         largest = lax.fori_loop(
-            0, 8, find_scores, jnp.full((8, BLOCK), masked_score, jnp.float32)
+            0, 8, find_scores, jnp.full((8, BLOCK), masked_score, jnp.float32), unroll=2
         )
         largest = jnp.max(largest, axis=0, keepdims=True)
 
@@ -241,23 +259,21 @@
             scratch[t] = e
             return total + folded(e, jnp.sum)
 
-        total = lax.fori_loop(0, 8, find_total, jnp.zeros((8, BLOCK), jnp.float32))
+        total = lax.fori_loop(0, 8, find_total, jnp.zeros((8, BLOCK), jnp.float32), unroll=2)
         inverse = 1.0 / jnp.sum(total, axis=0, keepdims=True)
 
         def divide(t, carry):
             weights[z, t] = (scratch[t] * inverse).astype(jnp.bfloat16)
             return carry
 
-        lax.fori_loop(0, 8, divide, 0)
+        lax.fori_loop(0, 8, divide, 0, unroll=2)
 
     level_loop(find_weights, 0, levels // 2)
-    share(VALUE, 2, values)
+    pass_on(VALUE, values)
     level_loop(find_weights, levels // 2, levels)
 
-    pass_on(VALUE, values)
-    await_bytes(qg.at[GRAD], in_recv.at[3])
-
     def find_value_terms(z):
+        await_bytes(qg.at[GRAD, z], in_recv.at[3, z])
         g = qg[GRAD, z]
 
         def own_tile(t, carry):
@@ -269,8 +285,8 @@
             pairs[VALUE, t // 2 - 1, z, tile_rows(t)] = term.astype(jnp.bfloat16)
             return carry
 
-        lax.fori_loop(0, 2, own_tile, 0)
-        lax.fori_loop(2, 8, far_tile, 0)
+        lax.fori_loop(0, 2, own_tile, 0, unroll=2)
+        lax.fori_loop(2, 8, far_tile, 0, unroll=2)
 
     level_loop(find_value_terms)
 
@@ -288,15 +304,20 @@
         for i in range(column_chunks):
 
             def add_rows(n, carry, i=i):
-                at = pl.ds(pl.multiple_of(chunk_start(i) + n * PIECE, PIECE), PIECE)
-                terms = pairs[which, :, :, at].reshape(TOPK * span, HD)
-                total = mm(choose[...], terms, ((1,), (0,)))
-                partial[which, :, :, at] = total.astype(jnp.bfloat16).reshape(
-                    RING, levels, PIECE, HD
-                )
+                first = chunk_start(i) + n * 2 * PIECE
+                both = [
+                    pl.ds(pl.multiple_of(first + m * PIECE, PIECE), PIECE) for m in range(2)
+                ]
+                terms = [pairs[which, :, :, at].reshape(TOPK * span, HD) for at in both]
+                total = mm(choose[...], jnp.concatenate(terms, axis=1), ((1,), (0,)))
+                total = total.astype(jnp.bfloat16)
+                for m, at in enumerate(both):
+                    partial[which, :, :, at] = total[:, m * HD : (m + 1) * HD].reshape(
+                        RING, levels, PIECE, HD
+                    )
                 return carry
 
-            lax.fori_loop(0, chunk // PIECE, add_rows, 0)
+            lax.fori_loop(0, chunk // (2 * PIECE), add_rows, 0)
             at = chunk_rows(i)
             for side, (part, to) in enumerate(((low, right), (high, left))):
                 ring_copy(
@@ -373,7 +394,7 @@
             scratch[t] = d
             return delta + folded(weights[z, t].astype(jnp.float32) * d, jnp.sum)
 
-        delta = lax.fori_loop(0, 8, find_dprobs, jnp.zeros((8, BLOCK), jnp.float32))
+        delta = lax.fori_loop(0, 8, find_dprobs, jnp.zeros((8, BLOCK), jnp.float32), unroll=2)
         delta = jnp.sum(delta, axis=0, keepdims=True)
 
         def find_terms(t, dq):
@@ -392,8 +413,8 @@
             pairs[KEY, t // 2 - 1, z, tile_rows(t)] = dk.astype(jnp.bfloat16)
             return dq
 
-        dq = lax.fori_loop(0, 2, own_tile, jnp.zeros((HD, BLOCK), jnp.float32))
-        dq = lax.fori_loop(2, 8, far_tile, dq)
+        dq = lax.fori_loop(0, 2, own_tile, jnp.zeros((HD, BLOCK), jnp.float32), unroll=2)
+        dq = lax.fori_loop(2, 8, far_tile, dq, unroll=2)
         done[0, z] = (dq.T * scaling).astype(jnp.bfloat16)
 
         def send_rows(k, carry):
@@ -402,17 +423,17 @@
 
         lax.fori_loop(0, nhead, send_rows, 0)
 
-    level_loop(find_key_terms, 0, levels // 2)
+    level_loop(find_key_terms, 0, levels // 2 - 1)
     send_sums(VALUE)
-    level_loop(find_key_terms, levels // 2, levels)
+    level_loop(find_key_terms, levels // 2 - 1, levels)
     send_terms(KEY)
+    finish(VALUE, v_out)
     send_sums(KEY)
-    finish(VALUE, v_out)
     finish(KEY, k_out)
 
     others_columns = pl.ds(0, (group - 1) * HD)
     await_bytes(lists.at[pl.ds(0, levels - 1)], list_send)
-    for which, src in enumerate((k_in, q_in, v_in, g_in)):
+    for which, src in enumerate((k_in, v_in, q_in, g_in)):
         await_bytes(src.at[:, others_columns], in_send.at[which])
     for which in range(2):
         for side in range(2):
@@ -456,7 +477,7 @@
         dma,
         dma,
         dma((4,)),
-        dma((4,)),
+        dma((4, levels)),
         dma((2, 4)),
         dma((2, 4)),
         dma((2, 4, nhead // 2)),

time: 238 us -> 210 us (0.88)
  Pallas kernels: 232 us -> 203 us
    pallas_call x1, Pallas kernels: 232 us -> 203 us  [per_device(): pl.pallas_call(functools.partial(kernel, levels, nhead), out_shape=(slab,...]
where the time goes in v3:
time: 210 us; the launch traced here: 209 us
  Pallas kernels  203 us (97%)
  local copies, waits for them, and re-layouts  4.93 us (2%)
    pallas_call x1, Pallas kernels, per_device(): pl.pallas_call(functools.partial(kernel, levels, nhead), out_shape=(slab,...  203 us
    unnamed x7, local copies, waits for them, and re-layouts  4.93 us

profile of v3, /device:TPU:1, one launch (start us, length us, event | category | flops | bytes accessed | tf_op | source)
XLA Modules:
  0.0 208.6 jit_solution(5048220238342843420)
XLA Ops:
  0.6 203.1 %sparse_attention_backward.1 = (bf16[64,8192]{1,0:T(8,128)(2,1)}, bf16[64,8192]{1,0:T(8,128)(2,1)}, bf16[64,8192]{1,0:T(8,128)(2,1)}) custom-call(bf16[64,8192]{1,0:T(8,128)(2,1)} %q_in.1, bf16[64,8192]{1,0:T(8,128)(2,1)} %k_in.1, bf16[64,8192]{1,0:T(8,128)(2,1)} %v_in.1, bf16[64,8192]{1,0:T(8,128)(2,1)} %g_in.1, s32[1,3]{1,0:T(1,128)} %chosen_ref.1), custom_call_target="tpu_custom_call" | custom-call | tf_op jit(solution)/shard_map/sparse_attention_backward/pallas_call | solution.py:488
  203.7 0.0 copy-start.1
  203.7 2.4 %copy.11 = bf16[64,8192]{1,0:T(8,128)(2,1)} copy(bf16[64,8192]{1,0:T(8,128)(2,1)} %get-tuple-element.6) | data formatting | bytes 2097152
  206.1 0.0 copy-done.1
  206.1 0.0 copy-start
  206.1 1.0 copy.12
  207.0 0.6 copy-done
  207.7 1.0 copy.13
Async XLA Ops:
  203.7 2.4 %copy-start.1 = (bf16[64,8192]{1,0:T(8,128)(2,1)S(1)}, bf16[64,8192]{1,0:T(8,128)(2,1)}, u32[]{:S(2)}) copy-start(bf16[64,8192]{1,0:T(8,128)(2,1)} %get-tuple-element.7) | copy-start | bytes 3145732
  206.1 1.6 copy-start

commit v4 on v3

--- a/solution.py
+++ b/solution.py
@@ -67,7 +67,7 @@
     z_me = c_me // RING
     x_me = lax.rem(c_me, RING)
     rows = BLOCK // nhead
-    column_chunks = nhead // 2
+    column_chunks = nhead
     chunk = BLOCK // column_chunks
     half = BLOCK // 2
     scaling = HD ** (-0.5)
@@ -250,7 +250,7 @@
             return jnp.maximum(largest, folded(s, jnp.max))
 
         largest = lax.fori_loop(
-            0, 8, find_scores, jnp.full((8, BLOCK), masked_score, jnp.float32), unroll=2
+            0, 8, find_scores, jnp.full((8, BLOCK), masked_score, jnp.float32), unroll=8
         )
         largest = jnp.max(largest, axis=0, keepdims=True)
 
@@ -259,14 +259,14 @@
             scratch[t] = e
             return total + folded(e, jnp.sum)
 
-        total = lax.fori_loop(0, 8, find_total, jnp.zeros((8, BLOCK), jnp.float32), unroll=2)
+        total = lax.fori_loop(0, 8, find_total, jnp.zeros((8, BLOCK), jnp.float32), unroll=8)
         inverse = 1.0 / jnp.sum(total, axis=0, keepdims=True)
 
         def divide(t, carry):
             weights[z, t] = (scratch[t] * inverse).astype(jnp.bfloat16)
             return carry
 
-        lax.fori_loop(0, 8, divide, 0, unroll=2)
+        lax.fori_loop(0, 8, divide, 0, unroll=8)
 
     level_loop(find_weights, 0, levels // 2)
     pass_on(VALUE, values)
@@ -286,16 +286,14 @@
             return carry
 
         lax.fori_loop(0, 2, own_tile, 0, unroll=2)
-        lax.fori_loop(2, 8, far_tile, 0, unroll=2)
+        lax.fori_loop(2, 8, far_tile, 0, unroll=6)
 
     level_loop(find_value_terms)
 
-    y_me = h_me // 2
-
     across = lax.rem(x_me + 2, RING)
 
     def chunk_start(i):
-        return lax.rem(y_me + i, column_chunks) * chunk
+        return lax.rem(h_me + i, column_chunks) * chunk
 
     def chunk_rows(i):
         return pl.ds(pl.multiple_of(chunk_start(i), chunk), chunk)
@@ -375,8 +373,7 @@
             level_loop(add_level)
 
             def send_level(z, i=i):
-                for n in range(2):
-                    send_out(1 + which, z, lax.rem(y_me + i, column_chunks) * 2 + n, dst)
+                send_out(1 + which, z, lax.rem(h_me + i, nhead), dst)
 
             level_loop(send_level)
 
@@ -394,7 +391,7 @@
             scratch[t] = d
             return delta + folded(weights[z, t].astype(jnp.float32) * d, jnp.sum)
 
-        delta = lax.fori_loop(0, 8, find_dprobs, jnp.zeros((8, BLOCK), jnp.float32), unroll=2)
+        delta = lax.fori_loop(0, 8, find_dprobs, jnp.zeros((8, BLOCK), jnp.float32), unroll=8)
         delta = jnp.sum(delta, axis=0, keepdims=True)
 
         def find_terms(t, dq):
@@ -414,7 +411,7 @@
             return dq
 
         dq = lax.fori_loop(0, 2, own_tile, jnp.zeros((HD, BLOCK), jnp.float32), unroll=2)
-        dq = lax.fori_loop(2, 8, far_tile, dq, unroll=2)
+        dq = lax.fori_loop(2, 8, far_tile, dq, unroll=6)
         done[0, z] = (dq.T * scaling).astype(jnp.bfloat16)
 
         def send_rows(k, carry):
@@ -480,8 +477,8 @@
         dma((4, levels)),
         dma((2, 4)),
         dma((2, 4)),
-        dma((2, 4, nhead // 2)),
-        dma((2, 4, nhead // 2)),
+        dma((2, 4, nhead)),
+        dma((2, 4, nhead)),
         dma((3,)),
         dma((3,)),
     ]

time: 210 us -> 202 us (0.962)
  Pallas kernels: 203 us -> 195 us
    pallas_call x1, Pallas kernels: 203 us -> 195 us  [per_device(): pl.pallas_call(functools.partial(kernel, levels, nhead), out_shape=(slab,...]
where the time goes in v4:
time: 202 us; the launch traced here: 201 us
  Pallas kernels  195 us (97%)
  local copies, waits for them, and re-layouts  4.93 us (2%)
    pallas_call x1, Pallas kernels, per_device(): pl.pallas_call(functools.partial(kernel, levels, nhead), out_shape=(slab,...  195 us
    unnamed x7, local copies, waits for them, and re-layouts  4.93 us

profile of v4, /device:TPU:1, one launch (start us, length us, event | category | flops | bytes accessed | tf_op | source)
XLA Modules:
  0.0 200.6 jit_solution(14990116611579032658)
XLA Ops:
  0.6 195.0 %sparse_attention_backward.1 = (bf16[64,8192]{1,0:T(8,128)(2,1)}, bf16[64,8192]{1,0:T(8,128)(2,1)}, bf16[64,8192]{1,0:T(8,128)(2,1)}) custom-call(bf16[64,8192]{1,0:T(8,128)(2,1)} %q_in.1, bf16[64,8192]{1,0:T(8,128)(2,1)} %k_in.1, bf16[64,8192]{1,0:T(8,128)(2,1)} %v_in.1, bf16[64,8192]{1,0:T(8,128)(2,1)} %g_in.1, s32[1,3]{1,0:T(1,128)} %chosen_ref.1), custom_call_target="tpu_custom_call" | custom-call | tf_op jit(solution)/shard_map/sparse_attention_backward/pallas_call | solution.py:485
  195.6 0.0 copy-start.1
  195.6 2.4 %copy.11 = bf16[64,8192]{1,0:T(8,128)(2,1)} copy(bf16[64,8192]{1,0:T(8,128)(2,1)} %get-tuple-element.6) | data formatting | bytes 2097152
  198.0 0.0 copy-done.1
  198.0 0.0 copy-start
  198.0 1.0 copy.12
  199.0 0.6 copy-done
  199.6 1.0 copy.13
Async XLA Ops:
  195.6 2.4 %copy-start.1 = (bf16[64,8192]{1,0:T(8,128)(2,1)S(1)}, bf16[64,8192]{1,0:T(8,128)(2,1)}, u32[]{:S(2)}) copy-start(bf16[64,8192]{1,0:T(8,128)(2,1)} %get-tuple-element.7) | copy-start | bytes 3145732
  198.0 1.6 copy-start

commit v5 on v4

--- a/solution.py
+++ b/solution.py
@@ -231,6 +231,13 @@
 
         lax.fori_loop(start, stop, step, 0)
 
+    def far_levels_first(body):
+        def step(k, carry):
+            body(near_level(levels - 1 - k))
+            return carry
+
+        lax.fori_loop(0, levels, step, 0)
+
     share(KEY, keys)
     pass_on(KEY, keys)
     share(VALUE, values)
@@ -325,25 +332,24 @@
                     to,
                 ).start()
 
-    def send_sums(which):
-        for i in range(column_chunks):
-            at = chunk_rows(i)
-            for side, (start, to) in enumerate(((0, right), (levels // 2, left))):
-                await_bytes(halves.at[which, side, :, at], part_recv.at[which, side, i])
-
-                def add_level(n, carry, at=at, side=side, start=start, to=to):
-                    both = partial[which, to, start + n, at].astype(jnp.float32)
-                    both = both + halves[which, side, n, at].astype(jnp.float32)
-                    partial[which, to, start + n, at] = both.astype(jnp.bfloat16)
-                    return carry
-
-                lax.fori_loop(0, levels // 2, add_level, 0)
-                ring_copy(
-                    partial.at[which, to, :, at],
-                    parts.at[which, side, :, at],
-                    (part_send.at[which, 2 + side, i], part_recv.at[which, 2 + side, i]),
-                    to,
-                ).start()
+    def send_sums(which, i):
+        at = chunk_rows(i)
+        for side, (start, to) in enumerate(((0, right), (levels // 2, left))):
+            await_bytes(halves.at[which, side, :, at], part_recv.at[which, side, i])
+
+            def add_level(n, carry, at=at, side=side, start=start, to=to):
+                both = partial[which, to, start + n, at].astype(jnp.float32)
+                both = both + halves[which, side, n, at].astype(jnp.float32)
+                partial[which, to, start + n, at] = both.astype(jnp.bfloat16)
+                return carry
+
+            lax.fori_loop(0, levels // 2, add_level, 0)
+            ring_copy(
+                partial.at[which, to, :, at],
+                parts.at[which, side, :, at],
+                (part_send.at[which, 2 + side, i], part_recv.at[which, 2 + side, i]),
+                to,
+            ).start()
 
     def send_out(which, z, h, dst):
         here = done.at[which, z, slab_rows(h)]
@@ -358,24 +364,23 @@
         def _():
             remote(here, there, out_send.at[which], out_recv.at[which], z, x_me, h).start()
 
-    def finish(which, dst):
-        for i in range(column_chunks):
-            at = chunk_rows(i)
+    def finish(which, dst, i):
+        at = chunk_rows(i)
+        for side in range(2):
+            await_bytes(parts.at[which, side, :, at], part_recv.at[which, 2 + side, i])
+
+        def add_level(z, at=at):
+            total = own[which, z, at] + partial[which, x_me, z, at].astype(jnp.float32)
             for side in range(2):
-                await_bytes(parts.at[which, side, :, at], part_recv.at[which, 2 + side, i])
-
-            def add_level(z, at=at):
-                total = own[which, z, at] + partial[which, x_me, z, at].astype(jnp.float32)
-                for side in range(2):
-                    total = total + parts[which, side, z, at].astype(jnp.float32)
-                done[1 + which, z, at] = total.astype(jnp.bfloat16)
-
-            level_loop(add_level)
-
-            def send_level(z, i=i):
-                send_out(1 + which, z, lax.rem(h_me + i, nhead), dst)
-
-            level_loop(send_level)
+                total = total + parts[which, side, z, at].astype(jnp.float32)
+            done[1 + which, z, at] = total.astype(jnp.bfloat16)
+
+        level_loop(add_level)
+
+        def send_level(z, i=i):
+            send_out(1 + which, z, lax.rem(h_me + i, nhead), dst)
+
+        far_levels_first(send_level)
 
     send_terms(VALUE)
 
@@ -420,13 +425,23 @@
 
         lax.fori_loop(0, nhead, send_rows, 0)
 
-    level_loop(find_key_terms, 0, levels // 2 - 1)
-    send_sums(VALUE)
-    level_loop(find_key_terms, levels // 2 - 1, levels)
+    def key_level(k, carry):
+        find_key_terms(near_level(k))
+
+        @pl.when(k == levels // 2 - 1)
+        def _():
+            for i in range(column_chunks):
+                send_sums(VALUE, i)
+
+        return carry
+
+    lax.fori_loop(0, levels, key_level, 0)
     send_terms(KEY)
-    finish(VALUE, v_out)
-    send_sums(KEY)
-    finish(KEY, k_out)
+    for i in range(column_chunks):
+        finish(VALUE, v_out, i)
+        send_sums(KEY, i)
+    for i in range(column_chunks):
+        finish(KEY, k_out, i)
 
     others_columns = pl.ds(0, (group - 1) * HD)
     await_bytes(lists.at[pl.ds(0, levels - 1)], list_send)

time: 202 us -> 201 us (level)
  no operation moved by 1% of the time
where the time goes in v5:
time: 201 us
  Pallas kernels  195 us (97%)
  local copies, waits for them, and re-layouts  4.93 us (2%)
    pallas_call x1, Pallas kernels, per_device(): pl.pallas_call(functools.partial(kernel, levels, nhead), out_shape=(slab,...  195 us
    unnamed x7, local copies, waits for them, and re-layouts  4.93 us

profile of v5, /device:TPU:1, one launch (start us, length us, event | category | flops | bytes accessed | tf_op | source)
XLA Modules:
  0.0 201.0 jit_solution(15518762240885377080)
XLA Ops:
  0.6 195.4 %sparse_attention_backward.1 = (bf16[64,8192]{1,0:T(8,128)(2,1)}, bf16[64,8192]{1,0:T(8,128)(2,1)}, bf16[64,8192]{1,0:T(8,128)(2,1)}) custom-call(bf16[64,8192]{1,0:T(8,128)(2,1)} %q_in.1, bf16[64,8192]{1,0:T(8,128)(2,1)} %k_in.1, bf16[64,8192]{1,0:T(8,128)(2,1)} %v_in.1, bf16[64,8192]{1,0:T(8,128)(2,1)} %g_in.1, s32[1,3]{1,0:T(1,128)} %chosen_ref.1), custom_call_target="tpu_custom_call" | custom-call | tf_op jit(solution)/shard_map/sparse_attention_backward/pallas_call | solution.py:500
  196.1 0.0 copy-start.1
  196.1 2.4 %copy.11 = bf16[64,8192]{1,0:T(8,128)(2,1)} copy(bf16[64,8192]{1,0:T(8,128)(2,1)} %get-tuple-element.6) | data formatting | bytes 2097152
  198.4 0.0 copy-done.1
  198.4 0.0 copy-start
  198.4 1.0 copy.12
  199.4 0.6 copy-done
  200.0 1.0 copy.13
Async XLA Ops:
  196.1 2.4 %copy-start.1 = (bf16[64,8192]{1,0:T(8,128)(2,1)S(1)}, bf16[64,8192]{1,0:T(8,128)(2,1)}, u32[]{:S(2)}) copy-start(bf16[64,8192]{1,0:T(8,128)(2,1)} %get-tuple-element.7) | copy-start | bytes 3145732
  198.4 1.6 copy-start
